TPU v7x, 32 devices: a whole 2x2x4 slice. The times are simulated.
32 devices in a mesh: dp: 4 (over y, x), mp: 8 (over z, core).
Axes of the slice: x: 2, y: 2, z: 4, core: 2. Of those that a mesh axis runs over, the one named last changes fastest.
Arguments:
- activations: bfloat16 [4096, 2048], P('dp', 'mp'), may hold values from -6 to 6
- out_grad: bfloat16 [4096, 8192], P('dp'), may hold values from -0.8984375 to 0.8984375
- old_weight: bfloat16 [8, 256, 8192], P('mp', 'dp'), may hold values from -0.125 to 0.125
- old_first: float32 [8, 256, 8192], P('mp', 'dp'), may hold values from -6 to 6
- old_second: float32 [8, 256, 8192], P('mp', 'dp'), may hold values from 0.25 to 4
- step: int32 [1], replicated, may hold values from 1 to 31
- next_input: bfloat16 [4096, 2048], P('dp', 'mp'), may hold values from -6 to 6
Outputs:
- new_weight: bfloat16 [8, 344, 8192], P('mp', 'dp')
- new_first: float32 [8, 344, 8192], P('mp', 'dp')
- new_second: float32 [8, 344, 8192], P('mp', 'dp')
- output: bfloat16 [4096, 8192], P('dp', 'mp')
Inputs may be any that keep to these rules, and one draw needn't show every extreme that they name: `step`: the number of Adam steps taken, this one included.
All inputs are finite; a program needn't handle non-finite values.
Results may differ from a plain program's by a relative error of at most 0.0049.
Values may be sent and summed in bfloat16 or wider, within the bound.
A program may use at most 192 MiB of HBM per device.

v0:
```python
import jax
import jax.numpy as jnp
from jax import lax
from jax.sharding import PartitionSpec as P


def from_behind(block, axis, distance):
    devices = range(lax.axis_size(axis))
    route = [(i - distance, i) for i in devices if i - distance in devices]
    return lax.ppermute(block, axis, route)


def body(activations, out_grad, old_weight, old_first, old_second, step, next_input):
    owners = lax.axis_size("dp")
    owner = lax.axis_index("dp")
    old_rows = old_weight.shape[1]
    width = old_weight.shape[2]
    held_rows = old_rows * owners
    shard_rows = (held_rows + owners - 2) // (owners - 1)
    padded_rows = owners * shard_rows
    tok_rows = activations.shape[0]
    moments = jnp.stack([old_first[0], old_second[0]])
    weight_next = from_behind(old_weight[0], "dp", -1)
    moment_next = from_behind(moments, "dp", -1)
    weight_rows = jnp.concatenate(
        [old_weight[0], weight_next, jnp.zeros((shard_rows, width), jnp.bfloat16)], 0
    )
    moment_rows = jnp.concatenate(
        [moments, moment_next, jnp.zeros((2, shard_rows, width), jnp.float32)], 1
    )
    begin = owner * (shard_rows - old_rows)
    weight_mine = lax.dynamic_slice_in_dim(weight_rows, begin, shard_rows, 0)
    moment_mine = lax.dynamic_slice_in_dim(moment_rows, begin, shard_rows, 1)
    row_index = owner * shard_rows + lax.broadcasted_iota(jnp.int32, (shard_rows, 1), 0)
    valid = row_index < held_rows
    feat_pad = jnp.concatenate(
        [activations, jnp.zeros((tok_rows, padded_rows - held_rows), jnp.bfloat16)], 1
    )
    grad = lax.psum_scatter(
        lax.dot_general(
            feat_pad, out_grad, (((0,), (0,)), ((), ())), preferred_element_type=jnp.float32
        ),
        "dp",
        scatter_dimension=0,
        tiled=True,
    )
    step_float = step[0].astype(jnp.float32)
    first_fix = 1.0 - jnp.power(jnp.float32(0.9), step_float)
    second_fix = 1.0 - jnp.power(jnp.float32(0.95), step_float)
    new_first = 0.9 * moment_mine[0] + 0.1 * grad
    new_second = 0.95 * moment_mine[1] + 0.05 * grad * grad
    safe_second = jnp.where(valid, new_second, jnp.float32(1.0))
    update = new_first / first_fix / (jnp.sqrt(safe_second / second_fix) + 1e-08)
    update = jnp.where(valid, update, jnp.float32(0.0))
    new_weight = (weight_mine.astype(jnp.float32) - 0.01 * update).astype(jnp.bfloat16)
    weight_all_new = lax.all_gather(new_weight, "dp", axis=0, tiled=True)[:held_rows]
    weight_cols = lax.all_to_all(weight_all_new, "mp", split_axis=1, concat_axis=0, tiled=True)
    input_all = lax.all_gather(next_input, "mp", axis=1, tiled=True)
    output = jnp.dot(input_all, weight_cols, preferred_element_type=jnp.float32).astype(
        jnp.bfloat16
    )
    return (new_weight[None], new_first[None], new_second[None], output)


def solution(mesh):
    return jax.shard_map(
        body,
        mesh=mesh,
        in_specs=(
            P("dp", "mp"),
            P("dp", None),
            P("mp", "dp", None),
            P("mp", "dp", None),
            P("mp", "dp", None),
            P(),
            P("dp", "mp"),
        ),
        out_specs=(P("mp", "dp", None), P("mp", "dp", None), P("mp", "dp", None), P("dp", "mp")),
        check_vma=False,
    )
```

profile of v0, /device:TPU:0, one launch (start us, length us, event | category | flops | bytes accessed | tf_op | source)
XLA Modules:
  0.0 492.6 jit_solution(16472965787498967166)
XLA Ops:
  7.2 0.0 all-gather.6.cloned.1.call-start
  7.2 3.2 constant_dynamic-update-slice_fusion.1
  10.4 1.5 constant_dynamic-update-slice_fusion
  11.9 1.3 collective-permute-start.1
  13.2 12.2 %fusion.10 = f32[344,8192]{1,0:T(8,128)} fusion(bf16[1024,8192]{1,0:T(8,128)(2,1)} %param.8, bf16[1024,256]{1,0:T(8,128)(2,1)S(1)} %copy-done.3), kind=kOutput, calls=%fused_computation.19 | convolution fusion | flops 5771362304 | bytes 28573696 | tf_op jit(solution)/shard_map/dot_general | solution.py:40
  25.4 190.4 %fusion = f32[96,8192]{1,0:T(8,128)S(1)} fusion(f32[344,8192]{1,0:T(8,128)} %fusion.10), kind=kCustom, calls=%all-reduce-scatter | all-reduce-scatter fusion | flops 3145729 | bytes 14418432
  215.8 1.0 slice.15
  216.8 4.7 collective-permute-start.2
  221.5 1.3 collective-permute-start
  223.5 0.6 dynamic-slice.6
  224.8 0.1 pad_dynamic-slice_fusion.4
  224.9 0.1 pad_dynamic-slice_fusion.5
  225.0 17.6 %collective-permute-done.2 = f32[30,8192]{1,0:T(8,128)} collective-permute-done((f32[30,8192]{1,0:T(8,128)}, f32[30,8192]{1,0:T(8,128)}, u32[]{:S(2)}, u32[]{:S(2)}) %collective-permute-start.2) | collective-permute-done | bytes 983072
  242.6 12.3 %concatenate.12 = f32[126,8192]{1,0:T(8,128)} concatenate(f32[30,8192]{1,0:T(8,128)} %collective-permute-done.2, f32[96,8192]{1,0:T(8,128)S(1)} %fusion), dimensions={0} | concatenate | bytes 8257536
  254.9 0.0 collective-permute-done.1
  254.9 4.4 fusion.2
  259.3 7.7 %collective-permute-done = bf16[64,8192]{1,0:T(8,128)(2,1)} collective-permute-done((bf16[64,8192]{1,0:T(8,128)(2,1)}, bf16[64,8192]{1,0:T(8,128)(2,1)}, u32[]{:S(2)}, u32[]{:S(2)}) %collective-permute-start) | collective-permute-done | bytes 1048608 | tf_op jit(solution)/shard_map/ppermute | solution.py:10
  267.0 5.9 %fusion.13 = (f32[1,86,8192]{2,1,0:T(8,128)S(1)}, f32[1,86,8192]{2,1,0:T(8,128)}, bf16[1,86,8192]{2,1,0:T(8,128)(2,1)}) fusion(f32[126,8192]{1,0:T(8,128)S(1)} %copy-done, u32[]{:S(6)} %subtract, f32[2,86,8192]{2,1,0:T(8,128)S(1)} %fusion.2, f32[]{:T(128)} %bitcast.4, f32[]{:T(128)} %bitcast.2, pred[86]{0:T(512)(128)(4,1)S(1)} %add_compare_fusion, ...), kind=kLoop, calls=%fused_computation.22 | loop fusion | flops 15499264 | bytes 17596690 | tf_op jit(solution)/shard_map/broadcast_in_dim | solution.py:62
  272.9 0.0 all-gather.6.cloned.1.call-update
  272.9 0.0 all-gather.4.cloned.1.call-start
  272.9 0.7 all-gather.4.cloned.1.call-update
  273.6 64.6 %all-gather.6.cloned.1.call-done = bf16[4,86,8192]{2,1,0:T(8,128)(2,1)} async-done(((bf16[1,86,8192]{2,1,0:T(8,128)(2,1)}), bf16[4,86,8192]{2,1,0:T(8,128)(2,1)}) %all-gather.6.cloned.1.call-update) | async-done | bytes 5636112 | tf_op jit(solution)/shard_map/all_gather | solution.py:56
  338.2 6.9 %reshape.32 = bf16[344,8192]{1,0:T(8,128)(2,1)} reshape(bf16[4,86,8192]{2,1,0:T(8,128)(2,1)} %all-gather.6.cloned.1.call-done) | data formatting | bytes 11272192
  345.1 2.4 slice-done
  347.5 2.4 copy.24
  349.9 4.7 all-to-all-start
  354.7 6.3 %copy.19 = f32[1,86,8192]{2,0,1:T(1,128)} copy(f32[1,86,8192]{2,1,0:T(8,128)} %get-tuple-element.17) | data formatting | bytes 5636096
  361.0 4.5 copy.20
  365.4 57.2 %all-gather.4.cloned.1.call-done = bf16[1024,2048]{1,0:T(8,128)(2,1)} async-done(((bf16[1024,256]{1,0:T(8,128)(2,1)}), bf16[1024,2048]{1,0:T(8,128)(2,1)}) %all-gather.4.cloned.1.call-update) | async-done | bytes 4194320 | tf_op jit(solution)/shard_map/all_gather | solution.py:58
  422.7 52.5 %all-to-all-done = bf16[256,8,1024]{2,0,1:T(8,128)(2,1)} async-done(((bf16[256,8,1024]{2,0,1:T(8,128)(2,1)}), bf16[256,8,1024]{2,0,1:T(8,128)(2,1)}, u32[]{:S(2)}, u32[]{:S(2)}) %all-to-all-start) | async-done | bytes 4194336 | tf_op jit(solution)/shard_map/all_to_all | solution.py:57
  475.2 8.0 %convert_bitcast_fusion = bf16[1024,1024]{0,1:T(8,128)(2,1)S(1)} fusion(bf16[2048,1024]{1,0:T(8,128)(2,1)} %bitcast.9, bf16[1024,2048]{1,0:T(8,128)(2,1)} %all-gather.4.cloned.1.call-done), kind=kOutput, calls=%fused_computation.15 | convolution fusion | flops 4296015872 | bytes 10485760 | tf_op jit(solution)/shard_map/dot_general | solution.py:59
  483.2 2.6 copy.21
  (14 shorter events, 0.0 us)
Async XLA Ops:
  7.2 3.2 copy-start.1
  7.2 331.0 %all-gather.6.cloned.1.call-start = ((), (), s32[]{:S(2)}) async-start(), calls=%async_computation.2 | async-start | bytes 7208960 | tf_op jit(solution)/shard_map/all_gather | solution.py:56
  10.4 2.8 copy-start.3
  11.9 243.0 %collective-permute-start.1 = (f32[2,64,8192]{2,1,0:T(8,128)}, f32[2,64,8192]{2,1,0:T(8,128)}, u32[]{:S(2)}, u32[]{:S(2)}) collective-permute-start(f32[2,64,8192]{2,1,0:T(8,128)} %constant_dynamic-update-slice_fusion), channel_id=1, source_target_pairs={{8,0},{16,8},{24,16},{9,1},{17,9},{25,17},{10,2},{18,10},{26,18},{... | collective-permute-start | bytes 12582920 | tf_op jit(solution)/shard_map/ppermute | solution.py:10
  25.4 198.2 %copy-start.4 = (u32[32]{0:T(128)S(1)}, u32[32]{0:T(128)}, u32[]{:S(2)}) copy-start(u32[32]{0:T(128)} %constant.51) | copy-start | bytes 388
  216.8 25.7 %collective-permute-start.2 = (f32[30,8192]{1,0:T(8,128)}, f32[30,8192]{1,0:T(8,128)}, u32[]{:S(2)}, u32[]{:S(2)}) collective-permute-start(f32[30,8192]{1,0:T(8,128)} %slice.15), channel_id=1, source_target_pairs={{0,8},{8,16},{16,24},{1,9},{9,17},{17,25},{2,10},{10,18},{18,26},{... | collective-permute-start | bytes 2949128
  221.5 45.5 %collective-permute-start = (bf16[64,8192]{1,0:T(8,128)(2,1)}, bf16[64,8192]{1,0:T(8,128)(2,1)}, u32[]{:S(2)}, u32[]{:S(2)}) collective-permute-start(bf16[64,8192]{1,0:T(8,128)(2,1)} %bitcast.42), channel_id=1, source_target_pairs={{8,0},{16,8},{24,16},{9,1},{17,9},{25,17},{10,2},{18,10},{26,18},{... | collective-permute-start | bytes 3145736 | tf_op jit(solution)/shard_map/ppermute | solution.py:10
  254.9 12.1 %copy-start = (f32[126,8192]{1,0:T(8,128)S(1)}, f32[126,8192]{1,0:T(8,128)}, u32[]{:S(2)}) copy-start(f32[126,8192]{1,0:T(8,128)} %concatenate.12) | copy-start | bytes 12386308
  254.9 12.1 %copy-start.2 = (bf16[1,64,8192]{2,1,0:T(8,128)(2,1)S(1)}, bf16[1,64,8192]{2,1,0:T(8,128)(2,1)}, u32[]{:S(2)}) copy-start(bf16[1,64,8192]{2,1,0:T(8,128)(2,1)} %param.9) | copy-start | bytes 3145732
  272.9 149.8 %all-gather.4.cloned.1.call-start = ((), (), s32[]{:S(2)}) async-start(), calls=%async_computation.1 | async-start | bytes 4718592 | tf_op jit(solution)/shard_map/all_gather | solution.py:58
  345.1 2.4 slice-start
  349.9 125.3 %all-to-all-start = ((bf16[256,8,1024]{2,0,1:T(8,128)(2,1)}), bf16[256,8,1024]{2,0,1:T(8,128)(2,1)}, u32[]{:S(2)}, u32[]{:S(2)}) async-start(bf16[256,8,1024]{2,0,1:T(8,128)(2,1)} %bitcast.41), calls=%async_computation | async-start | bytes 8388608 | tf_op jit(solution)/shard_map/all_to_all | solution.py:57
Sparse Core Ops, SparseCore 0:
  273.0 65.1 all-gather.5
  339.8 82.8 all-gather.3
where the time goes:
time: 494 us; the launch traced here: 493 us
  waiting for transfers between devices  200 us (40%)
  blocking collectives  190 us (38%)
  local copies, waits for them, and re-layouts  43.9 us (9%)
  matrix products  20.2 us (4%)
  between operations  15.5 us (3%)
  starting transfers between devices  12 us (2%)
  other arithmetic  10.3 us (2%)
    unnamed x1, blocking collectives  190 us
    all_gather x1, waiting for transfers between devices, body(): lax.all_gather(new_weight, 'dp', axis=0, tiled=True)[:held_rows]  64.6 us
    all_gather x1, waiting for transfers between devices, body(): input_all = lax.all_gather(next_input, 'mp', axis=1, tiled=True)  57.2 us
    all_to_all x1, waiting for transfers between devices, body(): lax.all_to_all(weight_all_new, 'mp', split_axis=1, concat_axis=0, tiled=T...  52.5 us
    unnamed x18, local copies, waits for them, and re-layouts  37.4 us
    unnamed x3, waiting for transfers between devices  18.3 us
    dot_general x1, matrix products, body(): lax.dot_general(feat_pad, out_grad, (((0,), (0,)), ((), ())), preferred_e...  12.2 us
  transfers between devices with their start and end apart: 6, of which 5 were waited for; matrix products, arithmetic and copies ran while one was open for 49% of the time, Pallas kernels for 0%

commit v1 on v0

--- a/solution.py
+++ b/solution.py
@@ -2,6 +2,16 @@
 import jax.numpy as jnp
 from jax import lax
 from jax.sharding import PartitionSpec as P
+
+
+def around_the_ring(value, name, along):
+    n_dev = lax.axis_size(name)
+    block, blocks = (value, [value])
+    for _ in range(n_dev - 1):
+        block = lax.ppermute(block, name, [(i, (i + 1) % n_dev) for i in range(n_dev)])
+        blocks.insert(0, block)
+    line = jnp.concatenate(blocks, axis=along)
+    return jnp.roll(line, (lax.axis_index(name) + 1) * value.shape[along], axis=along)
 
 
 def from_behind(block, axis, distance):
@@ -55,7 +65,7 @@
     new_weight = (weight_mine.astype(jnp.float32) - 0.01 * update).astype(jnp.bfloat16)
     weight_all_new = lax.all_gather(new_weight, "dp", axis=0, tiled=True)[:held_rows]
     weight_cols = lax.all_to_all(weight_all_new, "mp", split_axis=1, concat_axis=0, tiled=True)
-    input_all = lax.all_gather(next_input, "mp", axis=1, tiled=True)
+    input_all = around_the_ring(next_input, "mp", 1)
     output = jnp.dot(input_all, weight_cols, preferred_element_type=jnp.float32).astype(
         jnp.bfloat16
     )

time: 494 us -> 541 us (1.095); the launches traced: 493 us -> 533 us
  starting transfers between devices: 12 us -> 28.4 us
  waiting for transfers between devices: 200 us -> 216 us
  local copies, waits for them, and re-layouts: 43.9 us -> 50.6 us
    ppermute x0 -> x7, waiting for transfers between devices: none -> 125 us  [around_the_ring(): lax.ppermute(block, name, [(i, (i + 1) % n_dev) for i in range(n_dev)])]
    all_gather x1 -> x0, waiting for transfers between devices: 57.2 us -> none  [body(): input_all = lax.all_gather(next_input, 'mp', axis=1, tiled=True)]
    all_to_all x1, waiting for transfers between devices: 52.5 us -> 0.01 us  [body(): lax.all_to_all(weight_all_new, 'mp', split_axis=1, concat_axis=0, tiled=T...]
    ppermute x0 -> x7, starting transfers between devices: none -> 16.4 us  [around_the_ring(): lax.ppermute(block, name, [(i, (i + 1) % n_dev) for i in range(n_dev)])]
    unnamed x18 -> x58, local copies, waits for them, and re-layouts: 37.4 us -> 44.4 us
    unnamed x3 -> x2, waiting for transfers between devices: 18.3 us -> 17.6 us
  transfers between devices with their start and end apart: 6 -> 12, of which waited for: 5 -> 10; matrix products, arithmetic and copies ran while one was open for 49% -> 45% of each run, Pallas kernels for 0% -> 0%
where the time goes in v1:
time: 541 us; the launch traced here: 533 us
  waiting for transfers between devices  216 us (40%)
  blocking collectives  190 us (35%)
  local copies, waits for them, and re-layouts  50.6 us (9%)
  starting transfers between devices  28.4 us (5%)
  matrix products  21.4 us (4%)
  between operations  15.7 us (3%)
  other arithmetic  10.3 us (2%)
    unnamed x1, blocking collectives  190 us
    ppermute x7, waiting for transfers between devices, around_the_ring(): lax.ppermute(block, name, [(i, (i + 1) % n_dev) for i in range(n_dev)])  125 us
    all_gather x1, waiting for transfers between devices, body(): lax.all_gather(new_weight, 'dp', axis=0, tiled=True)[:held_rows]  65.3 us
    unnamed x58, local copies, waits for them, and re-layouts  44.4 us
    unnamed x2, waiting for transfers between devices  17.6 us
    ppermute x7, starting transfers between devices, around_the_ring(): lax.ppermute(block, name, [(i, (i + 1) % n_dev) for i in range(n_dev)])  16.4 us
    dot_general x1, matrix products, body(): lax.dot_general(feat_pad, out_grad, (((0,), (0,)), ((), ())), preferred_e...  12.2 us
  transfers between devices with their start and end apart: 12, of which 10 were waited for; matrix products, arithmetic and copies ran while one was open for 45% of the time, Pallas kernels for 0%

profile of v1, /device:TPU:0, one launch (start us, length us, event | category | flops | bytes accessed | tf_op | source)
XLA Modules:
  0.0 532.6 jit_solution(16846602032928018533)
XLA Ops:
  7.2 3.2 constant_dynamic-update-slice_fusion.1
  10.4 1.5 constant_dynamic-update-slice_fusion
  11.9 1.3 collective-permute-start.1
  13.2 12.2 %fusion.15 = f32[344,8192]{1,0:T(8,128)} fusion(bf16[1024,8192]{1,0:T(8,128)(2,1)} %param.8, bf16[1024,256]{1,0:T(8,128)(2,1)S(1)} %copy-done.15), kind=kOutput, calls=%fused_computation.21 | convolution fusion | flops 5771362304 | bytes 28573696 | tf_op jit(solution)/shard_map/dot_general | solution.py:50
  25.4 190.4 %fusion = f32[96,8192]{1,0:T(8,128)S(1)} fusion(f32[344,8192]{1,0:T(8,128)} %fusion.15), kind=kCustom, calls=%all-reduce-scatter | all-reduce-scatter fusion | flops 3145729 | bytes 14418432
  216.8 4.7 collective-permute-start.9
  221.5 1.3 collective-permute-start
  224.9 17.6 %collective-permute-done.9 = f32[30,8192]{1,0:T(8,128)} collective-permute-done((f32[30,8192]{1,0:T(8,128)}, f32[30,8192]{1,0:T(8,128)}, u32[]{:S(2)}, u32[]{:S(2)}) %collective-permute-start.9) | collective-permute-done | bytes 983072
  242.6 12.2 %concatenate.19 = f32[126,8192]{1,0:T(8,128)} concatenate(f32[30,8192]{1,0:T(8,128)} %collective-permute-done.9, f32[96,8192]{1,0:T(8,128)S(1)} %fusion), dimensions={0} | concatenate | bytes 8257536
  254.8 4.4 fusion.2
  259.1 7.8 %collective-permute-done = bf16[64,8192]{1,0:T(8,128)(2,1)} collective-permute-done((bf16[64,8192]{1,0:T(8,128)(2,1)}, bf16[64,8192]{1,0:T(8,128)(2,1)}, u32[]{:S(2)}, u32[]{:S(2)}) %collective-permute-start) | collective-permute-done | bytes 1048608 | tf_op jit(solution)/shard_map/ppermute | solution.py:20
  267.0 5.9 %fusion.18 = (f32[1,86,8192]{2,1,0:T(8,128)S(1)}, f32[1,86,8192]{2,1,0:T(8,128)}, bf16[1,86,8192]{2,1,0:T(8,128)(2,1)}) fusion(f32[126,8192]{1,0:T(8,128)S(1)} %copy-done, u32[]{:S(6)} %subtract.1, f32[2,86,8192]{2,1,0:T(8,128)S(1)} %fusion.2, f32[]{:T(128)} %bitcast.4, f32[]{:T(128)} %bitcast.2, pred[86]{0:T(512)(128)(4,1)S(1)} %add_compare_fusion, ...), kind=kLoop, calls=%fused_computation.24 | loop fusion | flops 15499264 | bytes 17596690 | tf_op jit(solution)/shard_map/broadcast_in_dim | solution.py:72
  272.9 65.3 %all-gather.3.cloned.1.call-done = bf16[4,86,8192]{2,1,0:T(8,128)(2,1)} async-done(((bf16[1,86,8192]{2,1,0:T(8,128)(2,1)}), bf16[4,86,8192]{2,1,0:T(8,128)(2,1)}) %all-gather.3.cloned.1.call-update) | async-done | bytes 5636112 | tf_op jit(solution)/shard_map/all_gather | solution.py:66
  338.2 6.9 %reshape.32 = bf16[344,8192]{1,0:T(8,128)(2,1)} reshape(bf16[4,86,8192]{2,1,0:T(8,128)(2,1)} %all-gather.3.cloned.1.call-done) | data formatting | bytes 11272192
  345.1 2.2 slice-done
  347.3 2.4 copy.21
  349.6 4.7 all-to-all-start
  354.9 77.7 %collective-permute-done.2 = bf16[1024,256]{1,0:T(8,128)(2,1)S(1)} collective-permute-done((bf16[1024,256]{1,0:T(8,128)(2,1)S(1)}, bf16[1024,256]{1,0:T(8,128)(2,1)S(1)}, u32[]{:S(2)}, u32[]{:S(2)}) %collective-permute-start.2) | collective-permute-done | bytes 524320 | tf_op jit(solution)/shard_map/ppermute | solution.py:11
  433.4 10.5 %collective-permute-done.3 = bf16[1024,256]{1,0:T(8,128)(2,1)S(1)} collective-permute-done((bf16[1024,256]{1,0:T(8,128)(2,1)S(1)}, bf16[1024,256]{1,0:T(8,128)(2,1)S(1)}, u32[]{:S(2)}, u32[]{:S(2)}) %collective-permute-start.3) | collective-permute-done | bytes 524320 | tf_op jit(solution)/shard_map/ppermute | solution.py:11
  444.7 10.5 %collective-permute-done.4 = bf16[1024,256]{1,0:T(8,128)(2,1)S(1)} collective-permute-done((bf16[1024,256]{1,0:T(8,128)(2,1)S(1)}, bf16[1024,256]{1,0:T(8,128)(2,1)S(1)}, u32[]{:S(2)}, u32[]{:S(2)}) %collective-permute-start.4) | collective-permute-done | bytes 524320 | tf_op jit(solution)/shard_map/ppermute | solution.py:11
  456.0 6.8 %collective-permute-start.5 = (bf16[1024,256]{1,0:T(8,128)(2,1)S(1)}, bf16[1024,256]{1,0:T(8,128)(2,1)S(1)}, u32[]{:S(2)}, u32[]{:S(2)}) collective-permute-start(bf16[1024,256]{1,0:T(8,128)(2,1)S(1)} %collective-permute-done.4), channel_id=1, source_target_pairs={{0,1},{1,2},{2,3},{3,4},{4,5},{5,6},{6,7},{7,0},{8,9},{9,10},{10,1... | collective-permute-start | bytes 1572872 | tf_op jit(solution)/shard_map/ppermute | solution.py:11
  462.7 3.7 collective-permute-done.5
  467.3 4.9 collective-permute-start.6
  472.1 5.5 %collective-permute-done.6 = bf16[1024,256]{1,0:T(8,128)(2,1)S(1)} collective-permute-done((bf16[1024,256]{1,0:T(8,128)(2,1)S(1)}, bf16[1024,256]{1,0:T(8,128)(2,1)S(1)}, u32[]{:S(2)}, u32[]{:S(2)}) %collective-permute-start.6) | collective-permute-done | bytes 524320 | tf_op jit(solution)/shard_map/ppermute | solution.py:11
  478.5 3.1 collective-permute-start.7
  481.5 7.4 %collective-permute-done.7 = bf16[1024,256]{1,0:T(8,128)(2,1)} collective-permute-done((bf16[1024,256]{1,0:T(8,128)(2,1)S(1)}, bf16[1024,256]{1,0:T(8,128)(2,1)}, u32[]{:S(2)}, u32[]{:S(2)}) %collective-permute-start.7) | collective-permute-done | bytes 524320 | tf_op jit(solution)/shard_map/ppermute | solution.py:11
  490.2 9.5 %collective-permute-done.8 = bf16[1024,256]{1,0:T(8,128)(2,1)} collective-permute-done((bf16[1024,256]{1,0:T(8,128)(2,1)}, bf16[1024,256]{1,0:T(8,128)(2,1)}, u32[]{:S(2)}, u32[]{:S(2)}) %collective-permute-start.8) | collective-permute-done | bytes 524320 | tf_op jit(solution)/shard_map/ppermute | solution.py:11
  501.9 1.2 constant_dynamic-update-slice_fusion.15
  504.6 1.3 constant_dynamic-update-slice_fusion.9
  507.5 4.5 copy.17
  512.0 4.5 copy.18
  516.4 9.3 %fusion.9 = bf16[1024,1024]{1,0:T(8,128)(2,1)} fusion(bf16[2048,1024]{1,0:T(8,128)(2,1)} %bitcast.9, bf16[1024,4096]{1,0:T(8,128)(2,1)} %copy-done.16, s32[]{:T(128)S(6)} %select_n.28), kind=kOutput, calls=%fused_computation.17 | convolution fusion | flops 4296015872 | bytes 10485764 | tf_op jit(solution)/shard_map/dot_general | solution.py:69
  (66 shorter events, 12.7 us)
Async XLA Ops:
  7.2 3.3 copy-start.2
  7.2 6.0 %copy-start.15 = (bf16[1024,256]{1,0:T(8,128)(2,1)S(1)}, bf16[1024,256]{1,0:T(8,128)(2,1)}, u32[]{:S(2)}) copy-start(bf16[1024,256]{1,0:T(8,128)(2,1)} %param.7) | copy-start | bytes 1572868
  7.2 331.0 %all-gather.3.cloned.1.call-start = ((), (), s32[]{:S(2)}) async-start(), calls=%async_computation.1 | async-start | bytes 7208960 | tf_op jit(solution)/shard_map/all_gather | solution.py:66
  11.9 242.9 %collective-permute-start.1 = (f32[2,64,8192]{2,1,0:T(8,128)}, f32[2,64,8192]{2,1,0:T(8,128)}, u32[]{:S(2)}, u32[]{:S(2)}) collective-permute-start(f32[2,64,8192]{2,1,0:T(8,128)} %constant_dynamic-update-slice_fusion), channel_id=1, source_target_pairs={{8,0},{16,8},{24,16},{9,1},{17,9},{25,17},{10,2},{18,10},{26,18},{... | collective-permute-start | bytes 12582920 | tf_op jit(solution)/shard_map/ppermute | solution.py:20
  25.4 198.2 %copy-start.17 = (u32[32]{0:T(128)S(1)}, u32[32]{0:T(128)}, u32[]{:S(2)}) copy-start(u32[32]{0:T(128)} %constant.78) | copy-start | bytes 388
  216.8 25.7 %collective-permute-start.9 = (f32[30,8192]{1,0:T(8,128)}, f32[30,8192]{1,0:T(8,128)}, u32[]{:S(2)}, u32[]{:S(2)}) collective-permute-start(f32[30,8192]{1,0:T(8,128)} %slice.15), channel_id=1, source_target_pairs={{0,8},{8,16},{16,24},{1,9},{9,17},{17,25},{2,10},{10,18},{18,26},{... | collective-permute-start | bytes 2949128
  221.5 45.5 %collective-permute-start = (bf16[64,8192]{1,0:T(8,128)(2,1)}, bf16[64,8192]{1,0:T(8,128)(2,1)}, u32[]{:S(2)}, u32[]{:S(2)}) collective-permute-start(bf16[64,8192]{1,0:T(8,128)(2,1)} %bitcast.39), channel_id=1, source_target_pairs={{8,0},{16,8},{24,16},{9,1},{17,9},{25,17},{10,2},{18,10},{26,18},{... | collective-permute-start | bytes 3145736 | tf_op jit(solution)/shard_map/ppermute | solution.py:20
  254.8 12.2 %copy-start = (f32[126,8192]{1,0:T(8,128)S(1)}, f32[126,8192]{1,0:T(8,128)}, u32[]{:S(2)}) copy-start(f32[126,8192]{1,0:T(8,128)} %concatenate.19) | copy-start | bytes 12386308
  254.8 12.2 %copy-start.14 = (bf16[1,64,8192]{2,1,0:T(8,128)(2,1)S(1)}, bf16[1,64,8192]{2,1,0:T(8,128)(2,1)}, u32[]{:S(2)}) copy-start(bf16[1,64,8192]{2,1,0:T(8,128)(2,1)} %param.9) | copy-start | bytes 3145732
  345.1 2.2 slice-start
  349.6 4.7 copy-start.3
  349.6 166.8 %all-to-all-start = ((bf16[256,8,1024]{2,0,1:T(8,128)(2,1)}), bf16[256,8,1024]{2,0,1:T(8,128)(2,1)}, u32[]{:S(2)}, u32[]{:S(2)}) async-start(bf16[256,8,1024]{2,0,1:T(8,128)(2,1)} %bitcast.38), calls=%async_computation | async-start | bytes 8388608 | tf_op jit(solution)/shard_map/all_to_all | solution.py:67
  354.4 78.2 %collective-permute-start.2 = (bf16[1024,256]{1,0:T(8,128)(2,1)S(1)}, bf16[1024,256]{1,0:T(8,128)(2,1)S(1)}, u32[]{:S(2)}, u32[]{:S(2)}) collective-permute-start(bf16[1024,256]{1,0:T(8,128)(2,1)S(1)} %copy-done.3), channel_id=1, source_target_pairs={{0,1},{1,2},{2,3},{3,4},{4,5},{5,6},{6,7},{7,0},{8,9},{9,10},{10,1... | collective-permute-start | bytes 1572872 | tf_op jit(solution)/shard_map/ppermute | solution.py:11
  432.6 0.8 copy-start.4
  433.4 10.5 %collective-permute-start.3 = (bf16[1024,256]{1,0:T(8,128)(2,1)S(1)}, bf16[1024,256]{1,0:T(8,128)(2,1)S(1)}, u32[]{:S(2)}, u32[]{:S(2)}) collective-permute-start(bf16[1024,256]{1,0:T(8,128)(2,1)S(1)} %collective-permute-done.2), channel_id=1, source_target_pairs={{0,1},{1,2},{2,3},{3,4},{4,5},{5,6},{6,7},{7,0},{8,9},{9,10},{10,1... | collective-permute-start | bytes 1572872 | tf_op jit(solution)/shard_map/ppermute | solution.py:11
  443.9 0.8 copy-start.6
  444.7 10.5 %collective-permute-start.4 = (bf16[1024,256]{1,0:T(8,128)(2,1)S(1)}, bf16[1024,256]{1,0:T(8,128)(2,1)S(1)}, u32[]{:S(2)}, u32[]{:S(2)}) collective-permute-start(bf16[1024,256]{1,0:T(8,128)(2,1)S(1)} %collective-permute-done.3), channel_id=1, source_target_pairs={{0,1},{1,2},{2,3},{3,4},{4,5},{5,6},{6,7},{7,0},{8,9},{9,10},{10,1... | collective-permute-start | bytes 1572872 | tf_op jit(solution)/shard_map/ppermute | solution.py:11
  455.2 0.8 copy-start.8
  456.0 10.5 %collective-permute-start.5 = (bf16[1024,256]{1,0:T(8,128)(2,1)S(1)}, bf16[1024,256]{1,0:T(8,128)(2,1)S(1)}, u32[]{:S(2)}, u32[]{:S(2)}) collective-permute-start(bf16[1024,256]{1,0:T(8,128)(2,1)S(1)} %collective-permute-done.4), channel_id=1, source_target_pairs={{0,1},{1,2},{2,3},{3,4},{4,5},{5,6},{6,7},{7,0},{8,9},{9,10},{10,1... | collective-permute-start | bytes 1572872 | tf_op jit(solution)/shard_map/ppermute | solution.py:11
  466.5 0.8 copy-start.10
  467.3 10.4 %collective-permute-start.6 = (bf16[1024,256]{1,0:T(8,128)(2,1)S(1)}, bf16[1024,256]{1,0:T(8,128)(2,1)S(1)}, u32[]{:S(2)}, u32[]{:S(2)}) collective-permute-start(bf16[1024,256]{1,0:T(8,128)(2,1)S(1)} %collective-permute-done.5), channel_id=1, source_target_pairs={{0,1},{1,2},{2,3},{3,4},{4,5},{5,6},{6,7},{7,0},{8,9},{9,10},{10,1... | collective-permute-start | bytes 1572872 | tf_op jit(solution)/shard_map/ppermute | solution.py:11
  477.7 0.8 copy-start.12
  478.5 10.5 %collective-permute-start.7 = (bf16[1024,256]{1,0:T(8,128)(2,1)S(1)}, bf16[1024,256]{1,0:T(8,128)(2,1)}, u32[]{:S(2)}, u32[]{:S(2)}) collective-permute-start(bf16[1024,256]{1,0:T(8,128)(2,1)S(1)} %collective-permute-done.6), channel_id=1, source_target_pairs={{0,1},{1,2},{2,3},{3,4},{4,5},{5,6},{6,7},{7,0},{8,9},{9,10},{10,1... | collective-permute-start | bytes 1572872 | tf_op jit(solution)/shard_map/ppermute | solution.py:11
  489.0 10.7 %collective-permute-start.8 = (bf16[1024,256]{1,0:T(8,128)(2,1)}, bf16[1024,256]{1,0:T(8,128)(2,1)}, u32[]{:S(2)}, u32[]{:S(2)}) collective-permute-start(bf16[1024,256]{1,0:T(8,128)(2,1)} %collective-permute-done.7), channel_id=1, source_target_pairs={{0,1},{1,2},{2,3},{3,4},{4,5},{5,6},{6,7},{7,0},{8,9},{9,10},{10,1... | collective-permute-start | bytes 1572872 | tf_op jit(solution)/shard_map/ppermute | solution.py:11
  490.1 14.2 %copy-start.9 = (bf16[1024,256]{1,0:T(8,128)(2,1)S(1)}, bf16[1024,256]{1,0:T(8,128)(2,1)}, u32[]{:S(2)}) copy-start(bf16[1024,256]{1,0:T(8,128)(2,1)} %copy-done.8) | copy-start | bytes 1572868
  490.1 14.2 %copy-start.7 = (bf16[1024,256]{1,0:T(8,128)(2,1)S(1)}, bf16[1024,256]{1,0:T(8,128)(2,1)}, u32[]{:S(2)}) copy-start(bf16[1024,256]{1,0:T(8,128)(2,1)} %copy-done.6) | copy-start | bytes 1572868
  490.1 14.3 %copy-start.5 = (bf16[1024,256]{1,0:T(8,128)(2,1)S(1)}, bf16[1024,256]{1,0:T(8,128)(2,1)}, u32[]{:S(2)}) copy-start(bf16[1024,256]{1,0:T(8,128)(2,1)} %copy-done.4) | copy-start | bytes 1572868
  501.9 5.1 copy-start.13
  503.1 4.0 copy-start.11
  504.6 2.9 copy-start.1
  507.4 4.5 copy-start.16
Sparse Core Ops, SparseCore 0:
  273.0 65.1 all-gather.2
